TPU v7x, 512 devices: a whole 4x4x16 slice. The times are simulated.
512 devices in a mesh: tm: 16 (over y, x), feat: 32 (over z, core).
Axes of the slice: x: 4, y: 4, z: 16, core: 2. Of those that a mesh axis runs over, the one named last changes fastest.
Arguments:
- bin_index: int32 [1024, 16384], P('feat', 'tm'), may hold values from 0 to 255
- node_ids: int32 [16384], P('tm'), may hold values from 0 to 31
- logits: float32 [16384], P(('tm', 'feat')), may hold values from -8 to 8
- labels: int32 [16384], P(('tm', 'feat')), may hold values 0 or 1
- roots: int32 [16], replicated, may hold values from 1 to 32
Outputs:
- split_gain: float32 [16, 32, 1024], P(None, None, 'feat')
- node_gain: float32 [16, 32], replicated
All inputs are finite; a program needn't handle non-finite values. No bound on the sum of `labels` on one device may be relied on, other than what follows from the above.
Results may differ from a plain program's by a relative error of at most 0.0021.
Values may be sent and summed in bfloat16 or wider, within the bound.
A program may use at most 128 MiB of HBM per device.

v0:
```python
import jax
import jax.numpy as jnp
from jax import lax
from jax.sharding import PartitionSpec as P

BINS = 256
NODES = 32
BLOCKS_DEV = 2
BLOCK_ROWS = 512


ridge = 1.0
group_width = 8


def prefix(array, axis, combine, identity):
    length, mine = (lax.axis_size(axis), lax.axis_index(axis))
    everything = lax.all_gather(array, axis)
    start = jnp.broadcast_to(jnp.asarray(identity, array.dtype), array.shape)

    def hop(k, before):
        reached = k < mine
        new = combine(before, everything[k])
        return jnp.where(reached, new, before)

    return lax.fori_loop(0, length, hop, start)


def best_gain(grad_sum, hess_sum):
    left_grad = jnp.cumsum(grad_sum, axis=-1)
    left_hess = jnp.cumsum(hess_sum, axis=-1)
    total_grad = left_grad[..., -1:]
    total_hess = left_hess[..., -1:]
    left_grad = left_grad[..., :-1]
    left_hess = left_hess[..., :-1]
    right_grad = total_grad - left_grad
    right_hess = total_hess - left_hess
    gains = (
        left_grad * left_grad / (left_hess + ridge)
        + right_grad * right_grad / (right_hess + ridge)
        - total_grad * total_grad / (total_hess + ridge)
    )
    return jnp.max(gains, axis=-1)


def add_sums(earlier, later):
    return earlier + later


def local(bin_index, node_ids, logits, labels, roots):
    probability = jax.nn.sigmoid(logits)
    gradient = (probability - labels.astype(jnp.float32)).astype(jnp.bfloat16)
    hessian = (probability * (1.0 - probability)).astype(jnp.bfloat16)
    gradient, hessian = (
        lax.all_gather(gradient, "feat", axis=0, tiled=True),
        lax.all_gather(hessian, "feat", axis=0, tiled=True),
    )
    feat_dev = bin_index.shape[0]
    row_block = min(512, BLOCK_ROWS)
    block_steps = BLOCK_ROWS // row_block
    node_hot = node_ids[:, None] == jnp.arange(NODES, dtype=jnp.int32)[None, :]
    weighted = jnp.concatenate(
        [
            jnp.where(node_hot, gradient[:, None], jnp.zeros((), jnp.bfloat16)),
            jnp.where(node_hot, hessian[:, None], jnp.zeros((), jnp.bfloat16)),
        ],
        axis=1,
    )
    bin_range = jnp.arange(BINS, dtype=jnp.int32)

    def block_hist(block_at):

        def add_rows(step_at, running_sum):
            offset = block_at * BLOCK_ROWS + step_at * row_block
            left_rows = lax.dynamic_slice_in_dim(weighted, offset, row_block, 0)
            columns = lax.dynamic_slice_in_dim(bin_index, offset, row_block, 1)
            pieces = []
            for group_at in range(feat_dev // group_width):
                chosen = columns[group_at * group_width : (group_at + 1) * group_width]
                bin_hot = (chosen[:, :, None] == bin_range).astype(jnp.bfloat16)
                pieces.append(
                    jnp.einsum(
                        "rc,frb->cfb", left_rows, bin_hot, preferred_element_type=jnp.float32
                    )
                )
            return running_sum + jnp.concatenate(pieces, axis=1)

        empty = jnp.zeros((2 * NODES, feat_dev, BINS), jnp.float32)
        return lax.fori_loop(0, block_steps, add_rows, empty)

    histograms = [block_hist(block_at) for block_at in range(BLOCKS_DEV)]
    own_index = lax.axis_index("tm")
    fold_count = roots.shape[0]
    own_total = histograms[0]
    block_at = 1
    own_total = own_total + histograms[block_at]
    earlier_sum = prefix(own_total, "tm", add_sums, jnp.zeros_like(own_total))
    local_index = roots - own_index * BLOCKS_DEV - 1
    picked = jnp.full((fold_count, NODES, feat_dev), -1e30, jnp.float32)
    running_hist = earlier_sum
    for block_at in range(BLOCKS_DEV):
        running_hist = running_hist + histograms[block_at]
        boundary_gain = best_gain(running_hist[:NODES], running_hist[NODES:])
        picked = jnp.where((local_index == block_at)[:, None, None], boundary_gain[None], picked)
    split_gain = lax.pmax(picked, "tm")
    node_gain = lax.pmax(jnp.max(split_gain, axis=2), "feat")
    return (split_gain, node_gain)


def solution(mesh):
    in_specs = (P("feat", "tm"), P("tm"), P(("tm", "feat")), P(("tm", "feat")), P())
    out_specs = (P(None, None, "feat"), P())
    return jax.shard_map(local, mesh=mesh, in_specs=in_specs, out_specs=out_specs, check_vma=False)
```

profile of v0, /device:TPU:1, one launch (start us, length us, event | category | flops | bytes accessed | tf_op | source)
XLA Modules:
  0.0 634.0 jit_solution(192854729711939372)
XLA Ops:
  8.7 1.3 dynamic-slice
  11.7 53.4 %all-reduce.2 = (bf16[1024]{0:T(1024)(128)(2,1)S(1)}, bf16[1024]{0:T(1024)(128)(2,1)S(1)}) all-reduce(bf16[1024]{0:T(1024)(128)(2,1)S(1)} %dynamic-update-slice, bf16[1024]{0:T(1024)(128)(2,1)S(1)} %dynamic-update-slice.1), channel_id=1, replica_groups=mesh['tm'=16,'feat'=32] {'feat'}, use_global_device_ids=true, to_apply=%add | all-reduce | flops 2048 | bytes 8192
  65.8 1.5 fusion
  67.4 1.5 fusion.1
  68.9 1.5 fusion.2
  70.4 1.5 fusion.3
  72.0 1.5 fusion.7
  73.5 1.5 fusion.4
  75.1 1.5 fusion.5
  76.6 1.5 fusion.6
  79.0 2.5 copy.31
  82.2 209.7 %all-gather.2.cloned.1.call-done = f32[16,64,32,256]{3,2,1,0:T(8,128)} async-done(((f32[1,64,32,256]{3,2,1,0:T(8,128)}), f32[16,64,32,256]{3,2,1,0:T(8,128)}) %all-gather.2.cloned.1.call-update) | async-done | bytes 33554448 | tf_op jit(solution)/shard_map/all_gather | solution.py:18
  291.9 37.3 %while.9 = (s32[]{:T(128)}, f32[64,32,256]{2,1,0:T(8,128)S(1)}, s32[]{:T(128)}, f32[16,64,32,256]{3,2,1,0:T(8,128)}, s32[]{:T(128)}, /*index=5*/s32[]{:T(128)}) while((s32[]{:T(128)}, f32[64,32,256]{2,1,0:T(8,128)S(1)}, s32[]{:T(128)}, f32[16,64,32,256]{3,2,1,0:T(8,128)}, s32[]{:T(128)}, /*index=5*/s32[]{:T(128)}) %tuple.62), condition=%wide.region_1.2_spmd.clone, body=%wide.region_0.1_spmd.clone.sunk | while | flops 1572868 | bytes 6291549 | solution.py:26
  291.9 2.3 add_select_fusion.2
  294.2 2.3 add_select_fusion.2
  296.5 2.3 add_select_fusion.2
  298.9 2.3 add_select_fusion.2
  301.2 2.3 add_select_fusion.2
  303.5 2.3 add_select_fusion.2
  305.9 2.3 add_select_fusion.2
  308.2 2.3 add_select_fusion.2
  310.6 2.3 add_select_fusion.2
  312.9 2.3 add_select_fusion.2
  315.2 2.3 add_select_fusion.2
  317.6 2.3 add_select_fusion.2
  319.9 2.3 add_select_fusion.2
  322.2 2.3 add_select_fusion.2
  324.6 2.3 add_select_fusion.2
  326.9 2.3 add_select_fusion.2
  329.2 3.3 maximum_add_fusion.2
  332.5 1.7 fusion.32
  335.4 18.4 %reduce-window.26 = f32[32,32,2,128]{3,1,2,0:T(8,128)S(1)} reduce-window(f32[32,32,2,128]{3,1,2,0:T(8,128)S(1)} %copy.33, f32[]{:T(128)} %constant.70.clone.1), window={size=1x1x1x128 pad=0_0x0_0x0_0x127_0}, to_apply=%region_2.3 | reduce-window | flops 33292288 | bytes 2097156 | tf_op jit(solution)/shard_map/reduce-window
  355.1 1.7 reshape.168
  357.5 18.4 %reduce-window.30 = f32[32,32,2,128]{3,1,2,0:T(8,128)S(1)} reduce-window(f32[32,32,2,128]{3,1,2,0:T(8,128)S(1)} %copy.37, f32[]{:T(128)} %constant.70.clone.1), window={size=1x1x1x128 pad=0_0x0_0x0_0x127_0}, to_apply=%region_4.5 | reduce-window | flops 33292288 | bytes 2097156 | tf_op jit(solution)/shard_map/reduce-window.2
  377.2 1.7 reshape.170
  378.9 1.6 copy.41
  380.5 32.3 %reduce-window.34 = f32[32,32,2,128]{3,1,2,0:T(8,128)S(1)} reduce-window(f32[32,32,2,128]{3,1,2,0:T(8,128)} %copy.41, f32[]{:T(128)} %constant.70.clone.1), window={size=1x1x1x128 pad=0_0x0_0x0_0x127_0}, to_apply=%region_7.8 | reduce-window | flops 33292288 | bytes 2097156 | tf_op jit(solution)/shard_map/reduce-window.4
  412.9 1.4 slice.143
  414.2 1.7 copy.42
  416.0 1.4 copy_bitcast_fusion.1
  417.4 1.7 reshape.172
  419.1 1.6 copy.45
  420.7 32.3 %reduce-window.36 = f32[32,32,2,128]{3,1,2,0:T(8,128)S(1)} reduce-window(f32[32,32,2,128]{3,1,2,0:T(8,128)} %copy.45, f32[]{:T(128)} %constant.70.clone.1), window={size=1x1x1x128 pad=0_0x0_0x0_0x127_0}, to_apply=%region_9.10 | reduce-window | flops 33292288 | bytes 2097156 | tf_op jit(solution)/shard_map/reduce-window.6
  453.1 1.3 slice.147
  454.4 1.7 copy.46
  460.7 113.8 %all-reduce.5.cloned.1.call-done = f32[16,32,32]{2,1,0:T(8,128)} async-done(((f32[16,32,32]{2,1,0:T(8,128)}), f32[16,32,32]{2,1,0:T(8,128)}) %all-reduce.5.cloned.1.call-update) | async-done | bytes 65552 | tf_op jit(solution)/shard_map/pmax | solution.py:105
  575.6 49.9 %pmax.15 = f32[16,32]{1,0:T(8,128)} all-reduce(f32[16,32]{1,0:T(8,128)S(1)} %reduce_max.29), channel_id=1, replica_groups=mesh['tm'=16,'feat'=32] {'feat'}, use_global_device_ids=true, to_apply=%region_14.15 | all-reduce | flops 512 | bytes 4096 | tf_op jit(solution)/shard_map/pmax | solution.py:106
  625.5 1.7 copy.68
  (60 shorter events, 14.7 us)
Async XLA Ops:
  7.2 284.7 %all-gather.2.cloned.1.call-start = ((), (), s32[]{:S(2)}) async-start(), calls=%async_computation | async-start | bytes 35651584 | tf_op jit(solution)/shard_map/all_gather | solution.py:18
  70.4 7.8 %copy-start.1 = (f32[64,8,256]{2,0,1:T(8,128)}, f32[64,8,256]{2,0,1:T(8,128)S(1)}, u32[]{:S(2)}) copy-start(f32[64,8,256]{2,0,1:T(8,128)S(1)} %fusion.2) | copy-start | bytes 1572868
  72.0 6.2 copy-start.2
  73.5 4.7 copy-start.3
  75.1 3.6 copy-start.4
  76.6 2.1 copy-start.5
  78.2 0.8 copy-start.6
  81.5 0.7 copy-start.7
  81.5 493.0 %all-reduce.5.cloned.1.call-start = ((), (), s32[]{:S(2)}) async-start(), calls=%async_computation.1 | async-start | bytes 524288 | tf_op jit(solution)/shard_map/pmax | solution.py:105
  456.0 1.5 copy-start
Sparse Core Ops, SparseCore 0:
  81.7 210.1 all-gather.1
  460.8 113.6 all-reduce.4
where the time goes:
time: 640 us; the launch traced here: 634 us
  waiting for transfers between devices  324 us (51%)
  other arithmetic  152 us (24%)
  blocking collectives  103 us (16%)
  local copies, waits for them, and re-layouts  27.1 us (4%)
  between operations  15.1 us (2%)
  matrix products  12.3 us (2%)
    all_gather x1, waiting for transfers between devices, prefix(): everything = lax.all_gather(array, axis)  210 us
    pmax x1, waiting for transfers between devices, local(): split_gain = lax.pmax(picked, 'tm')  114 us
    another operation x12, other arithmetic  104 us
    unnamed x1, blocking collectives  53.4 us
    pmax x1, blocking collectives, local(): node_gain = lax.pmax(jnp.max(split_gain, axis=2), 'feat')  49.9 us
    select_n x16, other arithmetic, hop(): return jnp.where(reached, new, before)  37 us
    another operation x22, local copies, waits for them, and re-layouts  16.8 us
  transfers between devices with their start and end apart: 2, of which 2 were waited for; matrix products, arithmetic and copies ran while one was open for 0% of the time, Pallas kernels for 0%

commit v1 on v0

v1 whole, which is shorter than its diff:
```python
import functools

import jax
import jax.numpy as jnp
from jax import lax
from jax.experimental import pallas as pl
from jax.experimental.pallas import tpu as pltpu
from jax.sharding import PartitionSpec as P

BINS = 256
NODES = 32
FOLDS = 16
LANES = 128
STEPS = 8
QUARTERS = 4
SUB = 4
MESH = pl.DeviceIdType.MESH
RIDGE = 1.0
F32 = jnp.float32
BF16 = jnp.bfloat16


def kernel(
    n_tm,
    n_feat,
    bins_ref,
    node_ref,
    logits_ref,
    labels_ref,
    roots_ref,
    split_ref,
    best_ref,
    send0,
    recv0,
    send1,
    recv1,
    send2,
    recv2,
    send4,
    recv4,
    send5,
    recv5,
    mask,
    sums,
    carry,
    gains,
    rolled,
    send_sems,
    recv_sems,
):
    tm = lax.axis_index("tm")
    feat = lax.axis_index("feat")

    def tm_peer(d):
        return lax.rem(tm + d, n_tm)

    def feat_peer(d):
        return lax.rem(feat + d, n_feat)

    barrier = pltpu.get_barrier_semaphore()
    for d in range(1, n_tm):
        pl.semaphore_signal(barrier, inc=1, device_id=(tm_peer(d), feat), device_id_type=MESH)
    for d in range(1, n_feat):
        pl.semaphore_signal(barrier, inc=1, device_id=(tm, feat_peer(d)), device_id_type=MESH)

    logits = jnp.concatenate([logits_ref[...]] * 4, axis=1)
    labels = jnp.concatenate([labels_ref[...]] * 4, axis=1).astype(F32)
    lane = lax.broadcasted_iota(jnp.int32, (1, LANES), 1)
    own = lane // 32 == lax.rem(feat, 4)
    prob = 1.0 / (1.0 + jnp.exp(-logits))
    grad = jnp.where(own, prob - labels, 0.0)
    hess = jnp.where(own, prob * (1.0 - prob), 0.0)
    send1[...] = jnp.concatenate([grad, hess], axis=0)

    nodes = node_ref[...].astype(F32)
    for t in range(n_tm):
        rows = []
        for f in (2 * t, 2 * t + 1):
            at = (f // 8) * 64 + f % 8
            rows.append(bins_ref[pl.ds(at, 8, stride=8), :].astype(F32))
        send0[t] = jnp.concatenate(rows + [nodes, nodes], axis=0).astype(BF16)

    pl.semaphore_wait(barrier, n_tm + n_feat - 2)

    def send(src, dst, phase, device):
        pltpu.make_async_remote_copy(
            src_ref=src,
            dst_ref=dst,
            send_sem=send_sems.at[phase],
            recv_sem=recv_sems.at[phase],
            device_id=device,
            device_id_type=MESH,
        ).start()

    def received(whole, phase):
        pltpu.make_async_copy(whole, whole, recv_sems.at[phase]).wait()

    def sent(part, phase):
        pltpu.make_async_copy(part, part, send_sems.at[phase]).wait()

    for d in range(1, n_feat):
        send(send1, recv1.at[feat], 1, (tm, feat_peer(d)))
    pltpu.make_async_copy(send1, recv1.at[feat], recv_sems.at[1]).start()
    for d in range(1, n_tm):
        send(send0.at[tm_peer(d)], recv0.at[tm], 0, (tm_peer(d), feat))
    pltpu.make_async_copy(send0.at[tm], recv0.at[tm], recv_sems.at[0]).start()

    received(recv1, 1)
    rows = []
    for s in range(8):
        rows.append((recv1[4 * s] + recv1[4 * s + 1]) + (recv1[4 * s + 2] + recv1[4 * s + 3]))
    send2[...] = jnp.concatenate(rows, axis=0).astype(BF16)

    for d in range(1, n_tm):
        send(send2, recv2.at[tm], 2, (tm_peer(d), feat))
    pltpu.make_async_copy(send2, recv2.at[tm], recv_sems.at[2]).start()

    received(recv0, 0)
    level = lax.broadcasted_iota(jnp.int32, (16, LANES), 0).astype(F32)
    one = jnp.ones((16, LANES), BF16)
    zero = jnp.zeros((16, LANES), BF16)

    def make_mask(i, _):
        half = lax.rem(i, 2)
        for j in range(QUARTERS):
            t = 4 * j + i // 2
            tile = recv0[t].astype(F32)
            for f in range(2):
                both = tile[8 * f : 8 * f + 8]
                four = jnp.where(half == 0, both[:4], both[4:])
                for s in range(SUB):
                    b16 = jnp.broadcast_to(four[s : s + 1], (16, LANES)).astype(BF16)
                    at = (j * SUB + s) * LANES
                    for v in range(BINS // 16):
                        cut = (level + 16.0 * v).astype(BF16)
                        mask[i, pl.ds(f * BINS + 16 * v, 16), pl.ds(at, LANES)] = jnp.where(
                            cut >= b16, one, zero
                        )
        return 0

    lax.fori_loop(0, STEPS, make_mask, 0)

    received(recv2, 2)
    node_level = lax.broadcasted_iota(jnp.int32, (NODES, LANES), 0).astype(F32)

    def accumulate(i, _):
        half = lax.rem(i, 2)
        quarters = []
        for j in range(QUARTERS):
            t = 4 * j + i // 2
            gh = recv2[t].astype(F32)
            gh = jnp.where(half == 0, gh[:8], gh[8:])
            node = recv0[t].astype(F32)[16:24]
            node = jnp.where(half == 0, node[:4], node[4:])
            grads, hesss = [], []
            for s in range(SUB):
                here = jnp.broadcast_to(node[s : s + 1], (NODES, LANES)) == node_level
                grads.append(jnp.where(here, jnp.broadcast_to(gh[2 * s : 2 * s + 1], (NODES, LANES)), 0.0).astype(BF16))
                hesss.append(jnp.where(here, jnp.broadcast_to(gh[2 * s + 1 : 2 * s + 2], (NODES, LANES)), 0.0).astype(BF16))
            grads = jnp.concatenate(grads, axis=1)
            hesss = jnp.concatenate(hesss, axis=1)
            pieces = []
            for kind in (grads, hesss):
                for q in range(QUARTERS):
                    pieces.append(kind if q == j else jnp.zeros_like(kind))
            quarters.append(jnp.concatenate(pieces, axis=0))
        weights = jnp.concatenate(quarters, axis=1)
        new = lax.dot_general(
            mask[i], weights, (((1,), (1,)), ((), ())), preferred_element_type=F32
        )

        @pl.when(i == 0)
        def _():
            sums[0] = new

        @pl.when(i > 0)
        def _():
            sums[i] = sums[jnp.maximum(i - 1, 0)] + new

        return 0

    lax.fori_loop(0, STEPS, accumulate, 0)

    wide = lax.broadcasted_iota(jnp.int32, (64, LANES), 1)

    def make_carry(c, _):
        at = pl.ds(pl.multiple_of(c * 64, 64), 64)
        for kind in range(2):
            cols = pl.ds(kind * LANES, LANES)
            total = sums[STEPS - 1, at, cols]
            shifted = jnp.where(wide >= 32, pltpu.roll(total, 32, 1), 0.0)
            acc = shifted + jnp.where(wide >= 64, pltpu.roll(total, 64, 1), 0.0)
            carry[at, cols] = acc + jnp.where(wide >= 96, pltpu.roll(total, 96, 1), 0.0)
        return 0

    lax.fori_loop(0, 8, make_carry, 0)

    chunk = 32
    last = lax.broadcasted_iota(jnp.int32, (chunk, LANES), 0) == chunk - 1

    def make_gains(i, _):
        for f in range(2):
            top = f * BINS + BINS - 1
            g_cols, h_cols = pl.ds(0, LANES), pl.ds(LANES, LANES)
            end = pl.ds(top, 1)
            g_all = sums[i, end, g_cols] + carry[end, g_cols]
            h_all = sums[i, end, h_cols] + carry[end, h_cols]
            best = None
            for c in range(BINS // chunk):
                at = pl.ds(f * BINS + c * chunk, chunk)
                g_left = sums[i, at, g_cols] + carry[at, g_cols]
                h_left = sums[i, at, h_cols] + carry[at, h_cols]
                g_right = g_all - g_left
                h_right = (h_all - h_left) + RIDGE
                h_left = h_left + RIDGE
                gain = (g_left * g_left * h_right + g_right * g_right * h_left) / (h_left * h_right)
                if c == BINS // chunk - 1:
                    gain = jnp.where(last, -jnp.inf, gain)
                best = gain if best is None else jnp.maximum(best, gain)
            best = jnp.max(best, axis=0, keepdims=True)
            gains[pl.ds(f * STEPS + i, 1), :] = best - g_all * g_all / (h_all + RIDGE)
        return 0

    lax.fori_loop(0, STEPS, make_gains, 0)

    for f in range(2):
        rows = gains[pl.ds(f * STEPS, STEPS), :]
        for r in range(QUARTERS):
            rolled[pl.ds(f * 32 + r * STEPS, STEPS), :] = rows if r == 0 else pltpu.roll(rows, 32 * r, 1)
    packed = []
    for f in range(2):
        for a in range(4):
            row = None
            for q in range(4):
                block = roots_ref[4 * q + a] - 1
                j = block // STEPS
                i = block - j * STEPS
                r = lax.rem(q - j + QUARTERS, QUARTERS)
                picked = rolled[pl.ds(f * 32 + r * STEPS + i, 1), :]
                row = picked if row is None else jnp.where(lane >= 32 * q, picked, row)
            packed.append(row)
    send4[...] = jnp.concatenate(packed, axis=0)

    mine = pl.ds(pl.multiple_of(tm * 8, 8), 8)
    for d in range(1, n_tm):
        send(send4, recv4.at[mine], 3, (tm_peer(d), feat))
    pltpu.make_async_copy(send4, recv4.at[mine], recv_sems.at[3]).start()
    received(recv4, 3)

    top = recv4[pl.ds(0, 8), :]
    for t in range(1, n_tm):
        top = jnp.maximum(top, recv4[pl.ds(8 * t, 8), :])
    send5[...] = jnp.maximum(top[:4], top[4:])
    for d in range(1, n_feat):
        send(send5, recv5.at[feat], 4, (tm, feat_peer(d)))
    pltpu.make_async_copy(send5, recv5.at[feat], recv_sems.at[4]).start()

    for a in range(4):
        turned = jnp.transpose(recv4[pl.ds(a, 2 * n_tm, stride=4), :])
        for q in range(4):
            split_ref[4 * q + a] = turned[32 * q : 32 * q + 32]

    sent(recv0.at[pl.ds(0, n_tm - 1)], 0)
    sent(recv1.at[pl.ds(0, n_feat - 1)], 1)
    sent(recv2.at[pl.ds(0, n_tm - 1)], 2)
    sent(recv4.at[pl.ds(0, 8 * (n_tm - 1))], 3)
    received(recv5, 4)
    top = recv5[0]
    for f in range(1, n_feat):
        top = jnp.maximum(top, recv5[f])
    for q in range(4):
        best_ref[pl.ds(4 * q, 4), :] = top[:, 32 * q : 32 * q + 32]
    sent(recv5.at[pl.ds(0, n_feat - 1)], 4)


def local(n_tm, n_feat, bin_index, node_ids, logits, labels, roots):
    bins = bin_index.reshape(4, 8, 8, LANES).transpose(0, 2, 1, 3).reshape(256, LANES)
    vmem = pl.BlockSpec(memory_space=pltpu.VMEM)
    smem = pl.BlockSpec(memory_space=pltpu.SMEM)
    return pl.pallas_call(
        functools.partial(kernel, n_tm, n_feat),
        out_shape=(
            jax.ShapeDtypeStruct((FOLDS, NODES, 2 * n_tm), F32),
            jax.ShapeDtypeStruct((FOLDS, NODES), F32),
        ),
        in_specs=[vmem, vmem, vmem, vmem, smem],
        out_specs=(vmem, vmem),
        scratch_shapes=[
            pltpu.VMEM((n_tm, 32, LANES), BF16),
            pltpu.VMEM((n_tm, 32, LANES), BF16),
            pltpu.VMEM((2, LANES), F32),
            pltpu.VMEM((n_feat, 2, LANES), F32),
            pltpu.VMEM((16, LANES), BF16),
            pltpu.VMEM((n_tm, 16, LANES), BF16),
            pltpu.VMEM((8, LANES), F32),
            pltpu.VMEM((8 * n_tm, LANES), F32),
            pltpu.VMEM((4, LANES), F32),
            pltpu.VMEM((n_feat, 4, LANES), F32),
            pltpu.VMEM((STEPS, 2 * BINS, QUARTERS * SUB * LANES), BF16),
            pltpu.VMEM((STEPS, 2 * BINS, 2 * LANES), F32),
            pltpu.VMEM((2 * BINS, 2 * LANES), F32),
            pltpu.VMEM((2 * STEPS, LANES), F32),
            pltpu.VMEM((2 * QUARTERS * STEPS, LANES), F32),
            pltpu.SemaphoreType.DMA((5,)),
            pltpu.SemaphoreType.DMA((5,)),
        ],
        compiler_params=pltpu.CompilerParams(
            collective_id=0, has_side_effects=True, vmem_limit_bytes=48 * 1024 * 1024
        ),
    )(bins, node_ids.reshape(8, LANES), logits.reshape(1, 32), labels.reshape(1, 32), roots)


def solution(mesh):
    in_specs = (P("feat", "tm"), P("tm"), P(("tm", "feat")), P(("tm", "feat")), P())
    out_specs = (P(None, None, "feat"), P())
    body = functools.partial(local, mesh.shape["tm"], mesh.shape["feat"])
    return jax.shard_map(body, mesh=mesh, in_specs=in_specs, out_specs=out_specs, check_vma=False)
```

time: 640 us -> 56.8 us (0.09)
  waiting for transfers between devices: 324 us -> 0 us
  other arithmetic: 152 us -> 0 us
  blocking collectives: 103 us -> 0 us
  Pallas kernels: 0 us -> 53.1 us
  local copies, waits for them, and re-layouts: 27.1 us -> 2.88 us
  between operations: 15.1 us -> 0.67 us
  matrix products: 12.3 us -> 0 us
    all_gather x1 -> x0, waiting for transfers between devices: 210 us -> none  [prefix(): everything = lax.all_gather(array, axis)]
    pmax x1 -> x0, waiting for transfers between devices: 114 us -> none  [local(): split_gain = lax.pmax(picked, 'tm')]
    another operation x12 -> x0, other arithmetic: 104 us -> none
    unnamed x1 -> x0, blocking collectives: 53.4 us -> none
    pallas_call x0 -> x1, Pallas kernels: none -> 53.1 us  [local(): pl.pallas_call(functools.partial(kernel, n_tm, n_feat), out_shape=(jax.Sh...]
    pmax x1 -> x0, blocking collectives: 49.9 us -> none  [local(): node_gain = lax.pmax(jnp.max(split_gain, axis=2), 'feat')]
    select_n x18 -> x0, other arithmetic: 38.5 us -> none  [the longest x16 37 us: hop(): return jnp.where(reached, new, before)]
    another operation x22 -> x0, local copies, waits for them, and re-layouts: 16.8 us -> none
  transfers between devices with their start and end apart: 2 -> 0, of which waited for: 2 -> 0; matrix products, arithmetic and copies ran while one was open for 0% -> 0% of each run, Pallas kernels for 0% -> 0%
where the time goes in v1:
time: 56.8 us; the launch traced here: 56.6 us
  Pallas kernels  53.1 us (93%)
  local copies, waits for them, and re-layouts  2.88 us (5%)
  between operations  0.67 us (1%)
    pallas_call x1, Pallas kernels, local(): pl.pallas_call(functools.partial(kernel, n_tm, n_feat), out_shape=(jax.Sh...  53.1 us
    unnamed x12, local copies, waits for them, and re-layouts  2.88 us

profile of v1, /device:TPU:1, one launch (start us, length us, event | category | flops | bytes accessed | tf_op | source)
XLA Modules:
  0.0 56.6 jit_solution(5587210461745635476)
XLA Ops:
  0.6 0.0 copy-start.1
  0.6 0.0 copy-start.2
  0.7 0.0 copy-start.3
  0.7 0.0 copy-start.4
  0.7 0.6 %copy-done.1 = s32[1024]{0:T(1024)S(1)} copy-done((s32[1024]{0:T(1024)S(1)}, s32[1024]{0:T(1024)}, u32[]{:S(2)}) %copy-start.1) | copy-done | bytes 4120
  1.3 0.0 copy-done.2
  1.3 0.0 copy-done.3
  1.3 0.0 copy-done.4
  1.3 0.0 copy-start
  1.3 0.9 %copy-done = s32[32,1024]{1,0:T(8,128)S(1)} copy-done((s32[32,1024]{1,0:T(8,128)S(1)}, s32[32,1024]{1,0:T(8,128)}, u32[]{:S(2)}) %copy-start) | copy-done | bytes 131096
  2.2 53.1 %shard_map.68 = (f32[16,32,32]{2,1,0:T(8,128)S(1)}, f32[16,32]{1,0:T(8,128)S(1)}) custom-call(s32[256,128]{1,0:T(8,128)S(1)} %bitcast.8, s32[8,128]{1,0:T(8,128)S(1)} %bitcast.9, f32[1,32]{1,0:T(1,128)S(1)} %bitcast.10, s32[1,32]{1,0:T(1,128)S(1)} %bitcast.11, s32[16]{0:T(128)S(1)} %copy-done.4), custom_call_target="tpu_custom_call" | custom-call | tf_op jit(solution)/shard_map/pallas_call | solution.py:280
  55.3 0.7 %copy.9 = f32[16,32,32]{2,1,0:T(8,128)} copy(f32[16,32,32]{2,1,0:T(8,128)S(1)} %get-tuple-element.4) | data formatting | bytes 131072
  56.0 0.6 %copy.10 = f32[16,32]{1,0:T(8,128)} copy(f32[16,32]{1,0:T(8,128)S(1)} %get-tuple-element.5) | data formatting | bytes 4096
Async XLA Ops:
  0.6 0.7 %copy-start.1 = (s32[1024]{0:T(1024)S(1)}, s32[1024]{0:T(1024)}, u32[]{:S(2)}) copy-start(s32[1024]{0:T(1024)} %param.6) | copy-start | bytes 12292
  0.6 0.7 %copy-start.2 = (f32[32]{0:T(128)S(1)}, f32[32]{0:T(128)}, u32[]{:S(2)}) copy-start(f32[32]{0:T(128)} %param.7) | copy-start | bytes 388
  0.7 0.7 %copy-start.3 = (s32[32]{0:T(128)S(1)}, s32[32]{0:T(128)}, u32[]{:S(2)}) copy-start(s32[32]{0:T(128)} %param.8) | copy-start | bytes 388
  0.7 0.7 %copy-start.4 = (s32[16]{0:T(128)S(1)}, s32[16]{0:T(128)}, u32[]{:S(2)}) copy-start(s32[16]{0:T(128)} %roots_ref.1) | copy-start | bytes 196
  1.3 0.9 %copy-start = (s32[32,1024]{1,0:T(8,128)S(1)}, s32[32,1024]{1,0:T(8,128)}, u32[]{:S(2)}) copy-start(s32[32,1024]{1,0:T(8,128)} %param.5) | copy-start | bytes 393220

commit v2 on v1

v2 whole, which is shorter than its diff:
```python
import functools

import jax
import jax.numpy as jnp
from jax import lax
from jax.experimental import pallas as pl
from jax.experimental.pallas import tpu as pltpu
from jax.sharding import PartitionSpec as P

BINS = 256
NODES = 32
FOLDS = 16
LANES = 128
STEPS = 8
QUARTERS = 4
SUBS = 8
MESH = pl.DeviceIdType.MESH
RIDGE = 1.0
UNROLL = 6
F32 = jnp.float32
BF16 = jnp.bfloat16


def kernel(
    n_tm,
    n_z,
    bins_hbm,
    node_hbm,
    logits_hbm,
    labels_hbm,
    roots_hbm,
    split_ref,
    best_ref,
    bins_ref,
    node_ref,
    logits_ref,
    labels_ref,
    roots_ref,
    fold_row,
    send0,
    recv0,
    send1,
    recv1,
    send2,
    recv2,
    send4,
    recv4,
    top4,
    recv_top,
    send5,
    recv5,
    mask,
    node_rows,
    sums,
    slope,
    total,
    grad_end,
    hess_end,
    gains,
    rolled,
    load_sems,
    send_sems,
    recv_sems,
    pair_sems,
    reach,
):
    tm = lax.axis_index("tm")
    feat = lax.axis_index("feat")
    z = feat // 2
    core = lax.rem(feat, 2)

    def tm_peer(d):
        return (lax.rem(tm + d, n_tm), feat)

    def tm_other(d):
        return (lax.rem(tm + d, n_tm), feat + 1 - 2 * core)

    def z_peer(d):
        return (tm, 2 * lax.rem(z + d, n_z) + core)

    z_order = sorted(range(1, n_z), key=lambda d: -min(d, n_z - d))
    near = n_z // 4
    peers = [tm_peer(d) for d in range(1, n_tm)] + [tm_other(d) for d in range(n_tm)]
    peers += [z_peer(d) for d in z_order if min(d, n_z - d) <= near]

    barrier = pltpu.get_barrier_semaphore()
    for peer in peers:
        pl.semaphore_signal(barrier, inc=1, device_id=peer, device_id_type=MESH)

    loads = [
        pltpu.make_async_copy(src, dst, load_sems.at[k])
        for k, (src, dst) in enumerate(
            [
                (logits_hbm, logits_ref),
                (labels_hbm, labels_ref),
                (bins_hbm, bins_ref),
                (node_hbm, node_ref),
                (roots_hbm, roots_ref),
            ]
        )
    ]
    for load in loads:
        load.start()

    loads[0].wait()
    loads[1].wait()
    logits = jnp.concatenate([logits_ref[...]] * 4, axis=1)
    labels = jnp.concatenate([labels_ref[...]] * 4, axis=1).astype(F32)
    lane = lax.broadcasted_iota(jnp.int32, (1, LANES), 1)
    place = core + 2 * lax.rem(z, 2)
    prob = 1.0 / (1.0 + jnp.exp(-logits))
    send1[...] = jnp.where(lane // 32 == place, prob - labels, 0.0) + jnp.where(
        lane // 32 == lax.rem(place + 2, 4), prob * (1.0 - prob), 0.0
    )

    loads[2].wait()
    loads[3].wait()
    nodes = node_ref[...].astype(F32)
    for t in range(n_tm):
        rows = []
        for f in (2 * t, 2 * t + 1):
            at = (f // 8) * 64 + f % 8
            rows.append(bins_ref[pl.ds(at, 8, stride=8), :].astype(F32))
        send0[t] = jnp.concatenate(rows + [nodes, nodes], axis=0).astype(BF16)

    pl.semaphore_wait(barrier, len(peers))
    pl.semaphore_signal(reach, inc=1, device_id=z_peer(near), device_id_type=MESH)
    pl.semaphore_signal(reach, inc=1, device_id=z_peer(n_z - near), device_id_type=MESH)

    def send(src, dst, send_sem, recv_sem, device):
        pltpu.make_async_remote_copy(
            src_ref=src,
            dst_ref=dst,
            send_sem=send_sem,
            recv_sem=recv_sem,
            device_id=device,
            device_id_type=MESH,
        ).start()

    def largest(rows):
        while len(rows) > 1:
            rest = rows[len(rows) // 2 * 2 :]
            rows = [jnp.maximum(a, b) for a, b in zip(rows[::2], rows[1::2])] + rest
        return rows[0]

    def wait(whole, sem):
        pltpu.make_async_copy(whole, whole, sem).wait()

    row = recv1.at[core * n_tm + tm]
    for d in range(1, n_tm):
        send(send1, row, send_sems.at[1], recv_sems.at[1], tm_peer(d))
    for d in range(n_tm):
        send(send1, row, send_sems.at[1], recv_sems.at[1], tm_other(d))
    pltpu.make_async_copy(send1, row, recv_sems.at[1]).start()
    for d in range(1, n_tm):
        device = tm_peer(d)
        send(send0.at[device[0]], recv0.at[tm], send_sems.at[0], recv_sems.at[0], device)
    pltpu.make_async_copy(send0.at[tm], recv0.at[tm], recv_sems.at[0]).start()

    def clear(i, _):
        sums[i] = jnp.zeros((2 * BINS, 2 * LANES), F32)
        return 0

    lax.fori_loop(0, STEPS, clear, 0)

    loads[4].wait()
    for o in range(FOLDS):
        block = roots_ref[o] - 1
        fold_row[o] = (((o // 4 - (block >> 3)) & 3) << 3) + (block & 7)

    wait(recv1, recv_sems.at[1])
    send2[...] = jnp.concatenate([recv1[t] + recv1[n_tm + t] for t in range(n_tm)], axis=0).astype(BF16)

    pl.semaphore_wait(reach, 2)
    for d in z_order:
        send(send2, recv2.at[z], send_sems.at[2], pair_sems.at[z // 2], z_peer(d))
    pltpu.make_async_copy(send2, recv2.at[z], pair_sems.at[z // 2]).start()

    wait(recv0, recv_sems.at[0])
    level = lax.broadcasted_iota(jnp.int32, (16, LANES), 0).astype(F32)
    one = jnp.ones((16, LANES), BF16)
    zero = jnp.zeros((16, LANES), BF16)

    def make_mask(tt, _):
        for j in range(QUARTERS):
            tile = recv0[4 * j + tt].astype(F32)
            for s in range(SUBS):
                node_rows[s, tt, pl.ds(j, 1), :] = tile[16 + s : 17 + s]
                for f in range(2):
                    b16 = jnp.broadcast_to(tile[8 * f + s : 8 * f + s + 1], (16, LANES)).astype(BF16)
                    for v in range(BINS // 16):
                        cut = (level + 16.0 * v).astype(BF16)
                        mask[s, tt, pl.ds(f * BINS + 16 * v, 16), pl.ds(j * LANES, LANES)] = jnp.where(
                            cut >= b16, one, zero
                        )
        return 0

    lax.fori_loop(0, 4, make_mask, 0)

    node_level = lax.broadcasted_iota(jnp.int32, (NODES, LANES), 0).astype(F32)
    low = lax.broadcasted_iota(jnp.int32, (16, LANES), 1) < 64
    blank = jnp.zeros((NODES, LANES), BF16)

    def accumulate(o, odd):
        near = (o + 1) // 2
        s = lax.rem(z // 2 + (near if odd else SUBS - near), SUBS)
        wait(recv2.at[pl.ds(2 * s, 2)], pair_sems.at[s])
        first = recv2[2 * s].astype(F32)
        second = recv2[2 * s + 1].astype(F32)
        grads = jnp.where(low, first, second)
        hesss = pltpu.roll(jnp.where(low, second, first), 64, 1)
        for tt in range(4):
            node = node_rows[s, tt]
            quarters = []
            for j in range(QUARTERS):
                t = 4 * j + tt
                here = jnp.broadcast_to(node[j : j + 1], (NODES, LANES)) == node_level
                pieces = []
                for kind in (grads, hesss):
                    chosen = jnp.where(here, jnp.broadcast_to(kind[t : t + 1], (NODES, LANES)), 0.0).astype(BF16)
                    pieces += [chosen if q == j else blank for q in range(QUARTERS)]
                quarters.append(jnp.concatenate(pieces, axis=0))
            weights = jnp.concatenate(quarters, axis=1)
            sums[2 * tt + s // 4] += lax.dot_general(
                mask[s, tt], weights, (((1,), (1,)), ((), ())), preferred_element_type=F32
            )
        return 0

    def accumulate_two(o, _):
        accumulate(2 * o, False)
        accumulate(2 * o + 1, True)
        return 0

    lax.fori_loop(0, SUBS // 2 - 1, accumulate_two, 0)
    accumulate(SUBS - 2, False)
    accumulate(SUBS - 1, True)

    lane8 = lax.broadcasted_iota(jnp.int32, (8, LANES), 1)
    kinds = (pl.ds(0, LANES), pl.ds(LANES, LANES))

    def prefixes(at):
        out = []
        for cols, ridge in zip(kinds, (0.0, RIDGE)):
            run = [sums[0, at, cols]]
            for i in range(1, STEPS):
                run.append(run[-1] + sums[i, at, cols])
            before = jnp.where(lane8 >= 32, pltpu.roll(run[-1], 32, 1), 0.0) + ridge
            before = before + jnp.where(lane8 >= 64, pltpu.roll(run[-1], 64, 1), 0.0)
            before = before + jnp.where(lane8 >= 96, pltpu.roll(run[-1], 96, 1), 0.0)
            out.append([r + before for r in run])
        return out

    last_row = lax.broadcasted_iota(jnp.int32, (8, LANES), 0) == 7
    for f in range(2):
        end = pl.ds(f * BINS + BINS - 8, 8)
        grads, hesss = prefixes(end)
        for i in range(STEPS):
            g_all = jnp.broadcast_to(grads[i][7:8], (8, LANES))
            s_all = jnp.broadcast_to(hesss[i][7:8], (8, LANES)) + RIDGE
            slope[i] = g_all / s_all
            total[i] = s_all
            grad_end[pl.ds(i, 1), :] = grads[i][7:8]
            hess_end[pl.ds(i, 1), :] = hesss[i][7:8]

        def chunk(at, drop):
            grads, hesss = prefixes(at)
            out = []
            for i in range(STEPS):
                a = hesss[i]
                apart = grads[i] - a * slope[i]
                product = a * (total[i] - a)
                inverse = pl.reciprocal(product, approx=True)
                inverse = inverse * (2.0 - product * inverse)
                gain = apart * apart * inverse
                out.append(jnp.where(last_row, 0.0, gain) if drop else gain)
            return out

        def scan(c, best):
            for k in range(UNROLL):
                at = pl.ds(pl.multiple_of(f * BINS + 8 * (UNROLL * c + k), 8), 8)
                best = [jnp.maximum(b, g) for b, g in zip(best, chunk(at, False))]
            return tuple(best)

        best = tuple(chunk(end, True))
        rounds = (BINS // 8 - 1) // UNROLL
        best = lax.fori_loop(0, rounds, scan, best)
        for c in range(rounds * UNROLL, BINS // 8 - 1):
            best = [jnp.maximum(b, g) for b, g in zip(best, chunk(pl.ds(f * BINS + 8 * c, 8), False))]
        best = jnp.concatenate([jnp.max(b, axis=0, keepdims=True) for b in best], axis=0)
        s_less = hess_end[...]
        g_all = grad_end[...]
        s_all = s_less + RIDGE
        gains[pl.ds(f * STEPS, STEPS), :] = s_all * best - g_all * g_all / (s_all * s_less)

    for f in range(2):
        rows = gains[pl.ds(f * STEPS, STEPS), :]
        for r in range(QUARTERS):
            rolled[pl.ds(f * 32 + r * STEPS, STEPS), :] = rows if r == 0 else pltpu.roll(rows, 32 * r, 1)
    packed = []
    for f in range(2):
        for a in range(4):
            row = None
            for q in range(4):
                picked = rolled[pl.ds(f * 32 + fold_row[4 * q + a], 1), :]
                row = picked if row is None else jnp.where(lane >= 32 * q, picked, row)
            packed.append(row)
    packed = jnp.concatenate(packed, axis=0)
    send4[...] = packed
    top4[...] = jnp.maximum(packed[:4], packed[4:])

    mine = pl.ds(pl.multiple_of(tm * 8, 8), 8)
    for d in range(1, n_tm):
        send(send4, recv4.at[mine], send_sems.at[3], recv_sems.at[3], tm_peer(d))
    for d in range(n_tm):
        send(top4, recv_top.at[tm], send_sems.at[4], recv_sems.at[4], tm_other(d))
    pltpu.make_async_copy(send4, recv4.at[mine], recv_sems.at[3]).start()
    wait(recv4, recv_sems.at[3])
    wait(recv_top, recv_sems.at[4])

    top = largest([recv4[pl.ds(8 * t, 8), :] for t in range(n_tm)])
    send5[...] = largest([top[:4], top[4:]] + [recv_top[t] for t in range(n_tm)])
    for d in z_order:
        send(send5, recv5.at[z], send_sems.at[5], recv_sems.at[5], z_peer(d))
    pltpu.make_async_copy(send5, recv5.at[z], recv_sems.at[5]).start()

    for a in range(4):
        turned = jnp.transpose(recv4[pl.ds(a, 2 * n_tm, stride=4), :])
        for q in range(4):
            split_ref[4 * q + a] = turned[32 * q : 32 * q + 32]

    wait(recv0.at[pl.ds(0, n_tm - 1)], send_sems.at[0])
    wait(recv1.at[pl.ds(0, 2 * n_tm - 1)], send_sems.at[1])
    wait(recv2.at[pl.ds(0, n_z - 1)], send_sems.at[2])
    wait(recv4.at[pl.ds(0, 8 * (n_tm - 1))], send_sems.at[3])
    wait(recv_top, send_sems.at[4])
    wait(recv5, recv_sems.at[5])
    top = largest([recv5[k] for k in range(n_z)])
    for q in range(4):
        best_ref[pl.ds(4 * q, 4), :] = top[:, 32 * q : 32 * q + 32]
    wait(recv5.at[pl.ds(0, n_z - 1)], send_sems.at[5])


def local(n_tm, n_feat, bin_index, node_ids, logits, labels, roots):
    n_z = n_feat // 2
    bins = bin_index.reshape(4, 8, 8, LANES).transpose(0, 2, 1, 3).reshape(256, LANES)
    operands = (bins, node_ids.reshape(8, LANES), logits.reshape(1, 32), labels.reshape(1, 32), roots)
    vmem = pl.BlockSpec(memory_space=pltpu.VMEM)
    hbm = pl.BlockSpec(memory_space=pltpu.HBM)
    return pl.pallas_call(
        functools.partial(kernel, n_tm, n_z),
        out_shape=(
            jax.ShapeDtypeStruct((FOLDS, NODES, 2 * n_tm), F32),
            jax.ShapeDtypeStruct((FOLDS, NODES), F32),
        ),
        in_specs=[hbm] * 5,
        out_specs=(vmem, vmem),
        scratch_shapes=[
            pltpu.VMEM((256, LANES), jnp.int32),
            pltpu.VMEM((8, LANES), jnp.int32),
            pltpu.VMEM((1, 32), F32),
            pltpu.VMEM((1, 32), jnp.int32),
            pltpu.SMEM((FOLDS,), jnp.int32),
            pltpu.SMEM((FOLDS,), jnp.int32),
            pltpu.VMEM((n_tm, 32, LANES), BF16),
            pltpu.VMEM((n_tm, 32, LANES), BF16),
            pltpu.VMEM((1, LANES), F32),
            pltpu.VMEM((2 * n_tm, 1, LANES), F32),
            pltpu.VMEM((n_tm, LANES), BF16),
            pltpu.VMEM((n_z, n_tm, LANES), BF16),
            pltpu.VMEM((8, LANES), F32),
            pltpu.VMEM((8 * n_tm, LANES), F32),
            pltpu.VMEM((4, LANES), F32),
            pltpu.VMEM((n_tm, 4, LANES), F32),
            pltpu.VMEM((4, LANES), F32),
            pltpu.VMEM((n_z, 4, LANES), F32),
            pltpu.VMEM((SUBS, 4, 2 * BINS, QUARTERS * LANES), BF16),
            pltpu.VMEM((SUBS, 4, QUARTERS, LANES), F32),
            pltpu.VMEM((STEPS, 2 * BINS, 2 * LANES), F32),
            pltpu.VMEM((STEPS, 8, LANES), F32),
            pltpu.VMEM((STEPS, 8, LANES), F32),
            pltpu.VMEM((STEPS, LANES), F32),
            pltpu.VMEM((STEPS, LANES), F32),
            pltpu.VMEM((2 * STEPS, LANES), F32),
            pltpu.VMEM((2 * QUARTERS * STEPS, LANES), F32),
            pltpu.SemaphoreType.DMA((5,)),
            pltpu.SemaphoreType.DMA((6,)),
            pltpu.SemaphoreType.DMA((6,)),
            pltpu.SemaphoreType.DMA((SUBS,)),
            pltpu.SemaphoreType.REGULAR,
        ],
        compiler_params=pltpu.CompilerParams(
            collective_id=0, has_side_effects=True, vmem_limit_bytes=32 * 1024 * 1024
        ),
    )(*[pltpu.with_memory_space_constraint(x, pltpu.HBM) for x in operands])


def solution(mesh):
    in_specs = (P("feat", "tm"), P("tm"), P(("tm", "feat")), P(("tm", "feat")), P())
    out_specs = (P(None, None, "feat"), P())
    body = functools.partial(local, mesh.shape["tm"], mesh.shape["feat"])
    return jax.shard_map(body, mesh=mesh, in_specs=in_specs, out_specs=out_specs, check_vma=False)
```

time: 56.8 us -> 46.4 us (0.82)
  Pallas kernels: 53.1 us -> 44.3 us
  local copies, waits for them, and re-layouts: 2.88 us -> 1.3 us
    pallas_call x1, Pallas kernels: 53.1 us -> 44.3 us  [local(): pl.pallas_call(functools.partial(kernel, n_tm, n_z), out_shape=(jax.Shape...]
    unnamed x12 -> x2, local copies, waits for them, and re-layouts: 2.88 us -> 1.3 us
where the time goes in v2:
time: 46.4 us; the launch traced here: 46.2 us
  Pallas kernels  44.3 us (95%)
  local copies, waits for them, and re-layouts  1.3 us (3%)
  between operations  0.64 us (1%)
    pallas_call x1, Pallas kernels, local(): pl.pallas_call(functools.partial(kernel, n_tm, n_z), out_shape=(jax.Shape...  44.3 us
    unnamed x2, local copies, waits for them, and re-layouts  1.3 us

profile of v2, /device:TPU:1, one launch (start us, length us, event | category | flops | bytes accessed | tf_op | source)
XLA Modules:
  0.0 46.2 jit_solution(13977462446371793855)
XLA Ops:
  0.6 44.3 %shard_map.68 = (f32[16,32,32]{2,1,0:T(8,128)S(1)}, f32[16,32]{1,0:T(8,128)S(1)}) custom-call(s32[256,128]{1,0:T(8,128)} %bitcast.8, s32[8,128]{1,0:T(8,128)} %bitcast.9, f32[1,32]{1,0:T(1,128)} %bitcast.10, s32[1,32]{1,0:T(1,128)} %bitcast.11, s32[16]{0:T(128)} %roots_hbm.1), custom_call_target="tpu_custom_call" | custom-call | tf_op jit(solution)/shard_map/pallas_call | solution.py:349
  44.9 0.7 %copy.9 = f32[16,32,32]{2,1,0:T(8,128)} copy(f32[16,32,32]{2,1,0:T(8,128)S(1)} %get-tuple-element.4) | data formatting | bytes 131072
  45.6 0.6 %copy.10 = f32[16,32]{1,0:T(8,128)} copy(f32[16,32]{1,0:T(8,128)S(1)} %get-tuple-element.5) | data formatting | bytes 4096

commit v3 on v2

--- a/solution.py
+++ b/solution.py
@@ -16,9 +16,38 @@
 SUBS = 8
 MESH = pl.DeviceIdType.MESH
 RIDGE = 1.0
-UNROLL = 6
+PAIR_ORDER = (
+    (0, 1, 2, 3, 7, 6, 5, 4),
+    (1, 0, 2, 3, 7, 6, 4, 5),
+    (2, 1, 3, 0, 4, 7, 5, 6),
+    (3, 2, 1, 0, 4, 5, 6, 7),
+    (4, 3, 5, 2, 6, 1, 0, 7),
+    (5, 4, 6, 3, 7, 2, 0, 1),
+    (6, 7, 5, 0, 4, 1, 3, 2),
+    (7, 0, 6, 1, 5, 2, 3, 4),
+)
+UNROLL = 8
 F32 = jnp.float32
 BF16 = jnp.bfloat16
+
+
+def largest(rows):
+    while len(rows) > 1:
+        rest = rows[len(rows) // 2 * 2 :]
+        rows = [jnp.maximum(a, b) for a, b in zip(rows[::2], rows[1::2])] + rest
+    return rows[0]
+
+
+def finish(split_ref, planes_ref, split_out, best_out, best_ref, sems):
+    copy = pltpu.make_async_copy(split_ref, split_out, sems.at[0])
+    copy.start()
+    top = largest([planes_ref[k] for k in range(planes_ref.shape[0])])
+    for q in range(4):
+        best_ref[pl.ds(4 * q, 4), :] = top[:, 32 * q : 32 * q + 32]
+    best_copy = pltpu.make_async_copy(best_ref, best_out, sems.at[1])
+    best_copy.start()
+    copy.wait()
+    best_copy.wait()
 
 
 def kernel(
@@ -30,7 +59,7 @@
     labels_hbm,
     roots_hbm,
     split_ref,
-    best_ref,
+    planes_ref,
     bins_ref,
     node_ref,
     logits_ref,
@@ -78,9 +107,13 @@
     def z_peer(d):
         return (tm, 2 * lax.rem(z + d, n_z) + core)
 
+    def away(d):
+        return min(d // 4, 4 - d // 4) + min(d % 4, 4 - d % 4)
+
+    tm_order = sorted(range(n_tm), key=lambda d: -away(d))
     z_order = sorted(range(1, n_z), key=lambda d: -min(d, n_z - d))
     near = n_z // 4
-    peers = [tm_peer(d) for d in range(1, n_tm)] + [tm_other(d) for d in range(n_tm)]
+    peers = [tm_other(d) for d in tm_order] + [tm_peer(d) for d in tm_order[:-1]]
     peers += [z_peer(d) for d in z_order if min(d, n_z - d) <= near]
 
     barrier = pltpu.get_barrier_semaphore()
@@ -137,22 +170,16 @@
             device_id_type=MESH,
         ).start()
 
-    def largest(rows):
-        while len(rows) > 1:
-            rest = rows[len(rows) // 2 * 2 :]
-            rows = [jnp.maximum(a, b) for a, b in zip(rows[::2], rows[1::2])] + rest
-        return rows[0]
-
     def wait(whole, sem):
         pltpu.make_async_copy(whole, whole, sem).wait()
 
     row = recv1.at[core * n_tm + tm]
-    for d in range(1, n_tm):
-        send(send1, row, send_sems.at[1], recv_sems.at[1], tm_peer(d))
-    for d in range(n_tm):
+    for d in tm_order:
         send(send1, row, send_sems.at[1], recv_sems.at[1], tm_other(d))
+        if d > 0:
+            send(send1, row, send_sems.at[1], recv_sems.at[1], tm_peer(d))
     pltpu.make_async_copy(send1, row, recv_sems.at[1]).start()
-    for d in range(1, n_tm):
+    for d in tm_order[:-1]:
         device = tm_peer(d)
         send(send0.at[device[0]], recv0.at[tm], send_sems.at[0], recv_sems.at[0], device)
     pltpu.make_async_copy(send0.at[tm], recv0.at[tm], recv_sems.at[0]).start()
@@ -172,7 +199,7 @@
     send2[...] = jnp.concatenate([recv1[t] + recv1[n_tm + t] for t in range(n_tm)], axis=0).astype(BF16)
 
     pl.semaphore_wait(reach, 2)
-    for d in z_order:
+    for d in z_order[::-1]:
         send(send2, recv2.at[z], send_sems.at[2], pair_sems.at[z // 2], z_peer(d))
     pltpu.make_async_copy(send2, recv2.at[z], pair_sems.at[z // 2]).start()
 
@@ -181,30 +208,36 @@
     one = jnp.ones((16, LANES), BF16)
     zero = jnp.zeros((16, LANES), BF16)
 
-    def make_mask(tt, _):
-        for j in range(QUARTERS):
-            tile = recv0[4 * j + tt].astype(F32)
-            for s in range(SUBS):
-                node_rows[s, tt, pl.ds(j, 1), :] = tile[16 + s : 17 + s]
-                for f in range(2):
-                    b16 = jnp.broadcast_to(tile[8 * f + s : 8 * f + s + 1], (16, LANES)).astype(BF16)
-                    for v in range(BINS // 16):
-                        cut = (level + 16.0 * v).astype(BF16)
-                        mask[s, tt, pl.ds(f * BINS + 16 * v, 16), pl.ds(j * LANES, LANES)] = jnp.where(
-                            cut >= b16, one, zero
-                        )
+    def make_mask(t, _):
+        j, tt = t // 4, lax.rem(t, 4)
+        tile = recv0[t].astype(F32)
+        at = pl.multiple_of(j * LANES, LANES)
+        for s in range(SUBS):
+            node_rows[s, tt, pl.ds(j, 1), :] = tile[16 + s : 17 + s]
+            for f in range(2):
+                b16 = jnp.broadcast_to(tile[8 * f + s : 8 * f + s + 1], (16, LANES)).astype(BF16)
+                for v in range(BINS // 16):
+                    cut = (level + 16.0 * v).astype(BF16)
+                    mask[s, tt, pl.ds(f * BINS + 16 * v, 16), pl.ds(at, LANES)] = jnp.where(cut >= b16, one, zero)
         return 0
 
-    lax.fori_loop(0, 4, make_mask, 0)
+    lax.fori_loop(0, n_tm, make_mask, 0)
 
     node_level = lax.broadcasted_iota(jnp.int32, (NODES, LANES), 0).astype(F32)
     low = lax.broadcasted_iota(jnp.int32, (16, LANES), 1) < 64
     blank = jnp.zeros((NODES, LANES), BF16)
 
-    def accumulate(o, odd):
-        near = (o + 1) // 2
-        s = lax.rem(z // 2 + (near if odd else SUBS - near), SUBS)
+    order = 0
+    for pair_at, row in enumerate(PAIR_ORDER):
+        code = sum(p << 3 * o for o, p in enumerate(row))
+        order = jnp.where(z // 2 == pair_at, code, order)
+
+    def pair(o):
+        s = (order >> 3 * o) & 7
         wait(recv2.at[pl.ds(2 * s, 2)], pair_sems.at[s])
+        return s
+
+    def accumulate(s):
         first = recv2[2 * s].astype(F32)
         second = recv2[2 * s + 1].astype(F32)
         grads = jnp.where(low, first, second)
@@ -224,16 +257,14 @@
             sums[2 * tt + s // 4] += lax.dot_general(
                 mask[s, tt], weights, (((1,), (1,)), ((), ())), preferred_element_type=F32
             )
+
+    def accumulate_two(o, _):
+        left, right = pair(2 * o), pair(2 * o + 1)
+        accumulate(left)
+        accumulate(right)
         return 0
 
-    def accumulate_two(o, _):
-        accumulate(2 * o, False)
-        accumulate(2 * o + 1, True)
-        return 0
-
-    lax.fori_loop(0, SUBS // 2 - 1, accumulate_two, 0)
-    accumulate(SUBS - 2, False)
-    accumulate(SUBS - 1, True)
+    lax.fori_loop(0, SUBS // 2, accumulate_two, 0)
 
     lane8 = lax.broadcasted_iota(jnp.int32, (8, LANES), 1)
     kinds = (pl.ds(0, LANES), pl.ds(LANES, LANES))
@@ -250,20 +281,21 @@
             out.append([r + before for r in run])
         return out
 
-    last_row = lax.broadcasted_iota(jnp.int32, (8, LANES), 0) == 7
-    for f in range(2):
-        end = pl.ds(f * BINS + BINS - 8, 8)
-        grads, hesss = prefixes(end)
+    row8 = lax.broadcasted_iota(jnp.int32, (8, LANES), 0)
+
+    def make_gains(f, _):
+        start = f * BINS
+        grads, hesss = prefixes(pl.ds(pl.multiple_of(start + BINS - 8, 8), 8))
         for i in range(STEPS):
-            g_all = jnp.broadcast_to(grads[i][7:8], (8, LANES))
             s_all = jnp.broadcast_to(hesss[i][7:8], (8, LANES)) + RIDGE
-            slope[i] = g_all / s_all
+            slope[i] = jnp.broadcast_to(grads[i][7:8], (8, LANES)) / s_all
             total[i] = s_all
             grad_end[pl.ds(i, 1), :] = grads[i][7:8]
             hess_end[pl.ds(i, 1), :] = hesss[i][7:8]
 
-        def chunk(at, drop):
-            grads, hesss = prefixes(at)
+        def chunk(c):
+            grads, hesss = prefixes(pl.ds(pl.multiple_of(start + 8 * c, 8), 8))
+            split = row8 < jnp.where(c == BINS // 8 - 1, 7, 8)
             out = []
             for i in range(STEPS):
                 a = hesss[i]
@@ -271,26 +303,24 @@
                 product = a * (total[i] - a)
                 inverse = pl.reciprocal(product, approx=True)
                 inverse = inverse * (2.0 - product * inverse)
-                gain = apart * apart * inverse
-                out.append(jnp.where(last_row, 0.0, gain) if drop else gain)
+                out.append(jnp.where(split, apart * apart * inverse, 0.0))
             return out
 
         def scan(c, best):
             for k in range(UNROLL):
-                at = pl.ds(pl.multiple_of(f * BINS + 8 * (UNROLL * c + k), 8), 8)
-                best = [jnp.maximum(b, g) for b, g in zip(best, chunk(at, False))]
+                best = [jnp.maximum(b, g) for b, g in zip(best, chunk(UNROLL * c + k))]
             return tuple(best)
 
-        best = tuple(chunk(end, True))
-        rounds = (BINS // 8 - 1) // UNROLL
-        best = lax.fori_loop(0, rounds, scan, best)
-        for c in range(rounds * UNROLL, BINS // 8 - 1):
-            best = [jnp.maximum(b, g) for b, g in zip(best, chunk(pl.ds(f * BINS + 8 * c, 8), False))]
+        best = tuple(jnp.zeros((8, LANES), F32) for _ in range(STEPS))
+        best = lax.fori_loop(0, BINS // 8 // UNROLL, scan, best)
         best = jnp.concatenate([jnp.max(b, axis=0, keepdims=True) for b in best], axis=0)
         s_less = hess_end[...]
         g_all = grad_end[...]
         s_all = s_less + RIDGE
-        gains[pl.ds(f * STEPS, STEPS), :] = s_all * best - g_all * g_all / (s_all * s_less)
+        gains[pl.ds(pl.multiple_of(f * STEPS, STEPS), STEPS), :] = s_all * best - g_all * g_all / (s_all * s_less)
+        return 0
+
+    lax.fori_loop(0, 2, make_gains, 0)
 
     for f in range(2):
         rows = gains[pl.ds(f * STEPS, STEPS), :]
@@ -309,20 +339,23 @@
     top4[...] = jnp.maximum(packed[:4], packed[4:])
 
     mine = pl.ds(pl.multiple_of(tm * 8, 8), 8)
-    for d in range(1, n_tm):
+    slot = recv_top.at[core * n_tm + tm]
+    for d in tm_order:
+        send(top4, slot, send_sems.at[4], recv_sems.at[4], tm_other(d))
+        if d > 0:
+            send(top4, slot, send_sems.at[4], recv_sems.at[4], tm_peer(d))
+    pltpu.make_async_copy(top4, slot, recv_sems.at[4]).start()
+    for d in tm_order[:-1]:
         send(send4, recv4.at[mine], send_sems.at[3], recv_sems.at[3], tm_peer(d))
-    for d in range(n_tm):
-        send(top4, recv_top.at[tm], send_sems.at[4], recv_sems.at[4], tm_other(d))
     pltpu.make_async_copy(send4, recv4.at[mine], recv_sems.at[3]).start()
-    wait(recv4, recv_sems.at[3])
     wait(recv_top, recv_sems.at[4])
 
-    top = largest([recv4[pl.ds(8 * t, 8), :] for t in range(n_tm)])
-    send5[...] = largest([top[:4], top[4:]] + [recv_top[t] for t in range(n_tm)])
+    send5[...] = largest([recv_top[k] for k in range(2 * n_tm)])
     for d in z_order:
         send(send5, recv5.at[z], send_sems.at[5], recv_sems.at[5], z_peer(d))
     pltpu.make_async_copy(send5, recv5.at[z], recv_sems.at[5]).start()
 
+    wait(recv4, recv_sems.at[3])
     for a in range(4):
         turned = jnp.transpose(recv4[pl.ds(a, 2 * n_tm, stride=4), :])
         for q in range(4):
@@ -332,11 +365,9 @@
     wait(recv1.at[pl.ds(0, 2 * n_tm - 1)], send_sems.at[1])
     wait(recv2.at[pl.ds(0, n_z - 1)], send_sems.at[2])
     wait(recv4.at[pl.ds(0, 8 * (n_tm - 1))], send_sems.at[3])
-    wait(recv_top, send_sems.at[4])
+    wait(recv_top.at[pl.ds(0, 2 * n_tm - 1)], send_sems.at[4])
     wait(recv5, recv_sems.at[5])
-    top = largest([recv5[k] for k in range(n_z)])
-    for q in range(4):
-        best_ref[pl.ds(4 * q, 4), :] = top[:, 32 * q : 32 * q + 32]
+    planes_ref[...] = recv5[...]
     wait(recv5.at[pl.ds(0, n_z - 1)], send_sems.at[5])
 
 
@@ -346,11 +377,11 @@
     operands = (bins, node_ids.reshape(8, LANES), logits.reshape(1, 32), labels.reshape(1, 32), roots)
     vmem = pl.BlockSpec(memory_space=pltpu.VMEM)
     hbm = pl.BlockSpec(memory_space=pltpu.HBM)
-    return pl.pallas_call(
+    split, planes = pl.pallas_call(
         functools.partial(kernel, n_tm, n_z),
         out_shape=(
             jax.ShapeDtypeStruct((FOLDS, NODES, 2 * n_tm), F32),
-            jax.ShapeDtypeStruct((FOLDS, NODES), F32),
+            jax.ShapeDtypeStruct((n_z, 4, LANES), F32),
         ),
         in_specs=[hbm] * 5,
         out_specs=(vmem, vmem),
@@ -370,7 +401,7 @@
             pltpu.VMEM((8, LANES), F32),
             pltpu.VMEM((8 * n_tm, LANES), F32),
             pltpu.VMEM((4, LANES), F32),
-            pltpu.VMEM((n_tm, 4, LANES), F32),
+            pltpu.VMEM((2 * n_tm, 4, LANES), F32),
             pltpu.VMEM((4, LANES), F32),
             pltpu.VMEM((n_z, 4, LANES), F32),
             pltpu.VMEM((SUBS, 4, 2 * BINS, QUARTERS * LANES), BF16),
@@ -392,6 +423,17 @@
             collective_id=0, has_side_effects=True, vmem_limit_bytes=32 * 1024 * 1024
         ),
     )(*[pltpu.with_memory_space_constraint(x, pltpu.HBM) for x in operands])
+    return pl.pallas_call(
+        finish,
+        out_shape=(
+            jax.ShapeDtypeStruct((FOLDS, NODES, 2 * n_tm), F32),
+            jax.ShapeDtypeStruct((FOLDS, NODES), F32),
+        ),
+        in_specs=[vmem, vmem],
+        out_specs=(hbm, hbm),
+        scratch_shapes=[pltpu.VMEM((FOLDS, NODES), F32), pltpu.SemaphoreType.DMA((2,))],
+        compiler_params=pltpu.CompilerParams(vmem_limit_bytes=4 * 1024 * 1024),
+    )(split, planes)
 
 
 def solution(mesh):

time: 46.4 us -> 43.6 us (0.940)
  Pallas kernels: 44.3 us -> 42.9 us
  local copies, waits for them, and re-layouts: 1.3 us -> 0 us
    pallas_call x1, Pallas kernels: 44.3 us -> 42.1 us  [local(): pl.pallas_call(functools.partial(kernel, n_tm, n_z), out_shape=(jax.Shape...]
    unnamed x2 -> x0, local copies, waits for them, and re-layouts: 1.3 us -> none
    pallas_call x0 -> x1, Pallas kernels: none -> 0.73 us  [local(): pl.pallas_call(finish, out_shape=(jax.ShapeDtypeStruct((FOLDS, NODES, 2 *...]
where the time goes in v3:
time: 43.6 us; the launch traced here: 43.5 us
  Pallas kernels  42.9 us (98%)
  between operations  0.64 us (1%)
    pallas_call x1, Pallas kernels, local(): pl.pallas_call(functools.partial(kernel, n_tm, n_z), out_shape=(jax.Shape...  42.1 us

profile of v3, /device:TPU:1, one launch (start us, length us, event | category | flops | bytes accessed | tf_op | source)
XLA Modules:
  0.0 43.5 jit_solution(3386966230493703085)
XLA Ops:
  0.6 42.1 %shard_map.68 = (f32[16,32,32]{2,1,0:T(8,128)S(1)}, f32[16,4,128]{2,1,0:T(4,128)S(1)}) custom-call(s32[256,128]{1,0:T(8,128)} %bitcast.8, s32[8,128]{1,0:T(8,128)} %bitcast.9, f32[1,32]{1,0:T(1,128)} %bitcast.10, s32[1,32]{1,0:T(1,128)} %bitcast.11, s32[16]{0:T(128)} %roots_hbm.1), custom_call_target="tpu_custom_call" | custom-call | tf_op jit(solution)/shard_map/pallas_call | solution.py:380
  42.8 0.7 %shard_map.69 = (f32[16,32,32]{2,1,0:T(8,128)}, f32[16,32]{1,0:T(8,128)}) custom-call(f32[16,32,32]{2,1,0:T(8,128)S(1)} %get-tuple-element.4.split_ref, f32[16,4,128]{2,1,0:T(4,128)S(1)} %get-tuple-element.5.planes_ref), custom_call_target="tpu_custom_call" | custom-call | tf_op jit(solution)/shard_map/pallas_call | solution.py:426

commit v4 on v3

--- a/solution.py
+++ b/solution.py
@@ -26,7 +26,7 @@
     (6, 7, 5, 0, 4, 1, 3, 2),
     (7, 0, 6, 1, 5, 2, 3, 4),
 )
-UNROLL = 8
+UNROLL = 32
 F32 = jnp.float32
 BF16 = jnp.bfloat16
 
@@ -322,29 +322,28 @@
 
     lax.fori_loop(0, 2, make_gains, 0)
 
-    for f in range(2):
-        rows = gains[pl.ds(f * STEPS, STEPS), :]
+    def fold_rows(k, rows):
         for r in range(QUARTERS):
-            rolled[pl.ds(f * 32 + r * STEPS, STEPS), :] = rows if r == 0 else pltpu.roll(rows, 32 * r, 1)
-    packed = []
-    for f in range(2):
+            rolled[pl.ds(k * 32 + r * STEPS, STEPS), :] = rows if r == 0 else pltpu.roll(rows, 32 * r, 1)
+        packed = []
         for a in range(4):
-            row = None
-            for q in range(4):
-                picked = rolled[pl.ds(f * 32 + fold_row[4 * q + a], 1), :]
-                row = picked if row is None else jnp.where(lane >= 32 * q, picked, row)
+            row = rolled[pl.ds(k * 32 + fold_row[a], 1), :]
+            for q in range(1, 4):
+                row = jnp.where(lane >= 32 * q, rolled[pl.ds(k * 32 + fold_row[4 * q + a], 1), :], row)
             packed.append(row)
-    packed = jnp.concatenate(packed, axis=0)
-    send4[...] = packed
-    top4[...] = jnp.maximum(packed[:4], packed[4:])
-
-    mine = pl.ds(pl.multiple_of(tm * 8, 8), 8)
+        return jnp.concatenate(packed, axis=0)
+
+    first, second = gains[pl.ds(0, STEPS), :], gains[pl.ds(STEPS, STEPS), :]
+    top4[...] = fold_rows(2, jnp.maximum(first, second))
     slot = recv_top.at[core * n_tm + tm]
     for d in tm_order:
         send(top4, slot, send_sems.at[4], recv_sems.at[4], tm_other(d))
         if d > 0:
             send(top4, slot, send_sems.at[4], recv_sems.at[4], tm_peer(d))
     pltpu.make_async_copy(top4, slot, recv_sems.at[4]).start()
+    send4[pl.ds(0, 4), :] = fold_rows(0, first)
+    send4[pl.ds(4, 4), :] = fold_rows(1, second)
+    mine = pl.ds(pl.multiple_of(tm * 8, 8), 8)
     for d in tm_order[:-1]:
         send(send4, recv4.at[mine], send_sems.at[3], recv_sems.at[3], tm_peer(d))
     pltpu.make_async_copy(send4, recv4.at[mine], recv_sems.at[3]).start()
@@ -412,7 +411,7 @@
             pltpu.VMEM((STEPS, LANES), F32),
             pltpu.VMEM((STEPS, LANES), F32),
             pltpu.VMEM((2 * STEPS, LANES), F32),
-            pltpu.VMEM((2 * QUARTERS * STEPS, LANES), F32),
+            pltpu.VMEM((3 * QUARTERS * STEPS, LANES), F32),
             pltpu.SemaphoreType.DMA((5,)),
             pltpu.SemaphoreType.DMA((6,)),
             pltpu.SemaphoreType.DMA((6,)),

time: 43.6 us -> 42.9 us (0.984)
  Pallas kernels: 42.9 us -> 42.1 us
    pallas_call x1, Pallas kernels: 42.1 us -> 41.3 us  [local(): pl.pallas_call(functools.partial(kernel, n_tm, n_z), out_shape=(jax.Shape...]
where the time goes in v4:
time: 42.9 us; the launch traced here: 42.7 us
  Pallas kernels  42.1 us (98%)
  between operations  0.64 us (1%)
    pallas_call x1, Pallas kernels, local(): pl.pallas_call(functools.partial(kernel, n_tm, n_z), out_shape=(jax.Shape...  41.3 us

profile of v4, /device:TPU:1, one launch (start us, length us, event | category | flops | bytes accessed | tf_op | source)
XLA Modules:
  0.0 42.7 jit_solution(11549079313986310799)
XLA Ops:
  0.6 41.3 %shard_map.68 = (f32[16,32,32]{2,1,0:T(8,128)S(1)}, f32[16,4,128]{2,1,0:T(4,128)S(1)}) custom-call(s32[256,128]{1,0:T(8,128)} %bitcast.8, s32[8,128]{1,0:T(8,128)} %bitcast.9, f32[1,32]{1,0:T(1,128)} %bitcast.10, s32[1,32]{1,0:T(1,128)} %bitcast.11, s32[16]{0:T(128)} %roots_hbm.1), custom_call_target="tpu_custom_call" | custom-call | tf_op jit(solution)/shard_map/pallas_call | solution.py:379
  42.0 0.7 %shard_map.69 = (f32[16,32,32]{2,1,0:T(8,128)}, f32[16,32]{1,0:T(8,128)}) custom-call(f32[16,32,32]{2,1,0:T(8,128)S(1)} %get-tuple-element.4.split_ref, f32[16,4,128]{2,1,0:T(4,128)S(1)} %get-tuple-element.5.planes_ref), custom_call_target="tpu_custom_call" | custom-call | tf_op jit(solution)/shard_map/pallas_call | solution.py:425

commit v5 on v4

--- a/solution.py
+++ b/solution.py
@@ -78,8 +78,8 @@
     recv_top,
     send5,
     recv5,
-    mask,
-    node_rows,
+    rows32,
+    cuts,
     sums,
     slope,
     total,
@@ -195,6 +195,7 @@
         block = roots_ref[o] - 1
         fold_row[o] = (((o // 4 - (block >> 3)) & 3) << 3) + (block & 7)
 
+    cuts[...] = lax.broadcasted_iota(jnp.int32, (BINS, LANES), 0).astype(F32).astype(BF16)
     wait(recv1, recv_sems.at[1])
     send2[...] = jnp.concatenate([recv1[t] + recv1[n_tm + t] for t in range(n_tm)], axis=0).astype(BF16)
 
@@ -204,24 +205,22 @@
     pltpu.make_async_copy(send2, recv2.at[z], pair_sems.at[z // 2]).start()
 
     wait(recv0, recv_sems.at[0])
-    level = lax.broadcasted_iota(jnp.int32, (16, LANES), 0).astype(F32)
+    for t in range(n_tm):
+        rows32[t] = recv0[t].astype(F32)[:24]
     one = jnp.ones((16, LANES), BF16)
     zero = jnp.zeros((16, LANES), BF16)
 
-    def make_mask(t, _):
-        j, tt = t // 4, lax.rem(t, 4)
-        tile = recv0[t].astype(F32)
-        at = pl.multiple_of(j * LANES, LANES)
-        for s in range(SUBS):
-            node_rows[s, tt, pl.ds(j, 1), :] = tile[16 + s : 17 + s]
+    def mask(s, tt):
+        columns = []
+        for j in range(QUARTERS):
+            tiles = []
             for f in range(2):
-                b16 = jnp.broadcast_to(tile[8 * f + s : 8 * f + s + 1], (16, LANES)).astype(BF16)
+                row = rows32[4 * j + tt, pl.ds(8 * f + s, 1), :]
+                b16 = jnp.broadcast_to(row, (16, LANES)).astype(BF16)
                 for v in range(BINS // 16):
-                    cut = (level + 16.0 * v).astype(BF16)
-                    mask[s, tt, pl.ds(f * BINS + 16 * v, 16), pl.ds(at, LANES)] = jnp.where(cut >= b16, one, zero)
-        return 0
-
-    lax.fori_loop(0, n_tm, make_mask, 0)
+                    tiles.append(jnp.where(cuts[pl.ds(16 * v, 16), :] >= b16, one, zero))
+            columns.append(jnp.concatenate(tiles, axis=0))
+        return jnp.concatenate(columns, axis=1)
 
     node_level = lax.broadcasted_iota(jnp.int32, (NODES, LANES), 0).astype(F32)
     low = lax.broadcasted_iota(jnp.int32, (16, LANES), 1) < 64
@@ -243,11 +242,10 @@
         grads = jnp.where(low, first, second)
         hesss = pltpu.roll(jnp.where(low, second, first), 64, 1)
         for tt in range(4):
-            node = node_rows[s, tt]
             quarters = []
             for j in range(QUARTERS):
                 t = 4 * j + tt
-                here = jnp.broadcast_to(node[j : j + 1], (NODES, LANES)) == node_level
+                here = jnp.broadcast_to(rows32[t, pl.ds(16 + s, 1), :], (NODES, LANES)) == node_level
                 pieces = []
                 for kind in (grads, hesss):
                     chosen = jnp.where(here, jnp.broadcast_to(kind[t : t + 1], (NODES, LANES)), 0.0).astype(BF16)
@@ -255,7 +253,7 @@
                 quarters.append(jnp.concatenate(pieces, axis=0))
             weights = jnp.concatenate(quarters, axis=1)
             sums[2 * tt + s // 4] += lax.dot_general(
-                mask[s, tt], weights, (((1,), (1,)), ((), ())), preferred_element_type=F32
+                mask(s, tt), weights, (((1,), (1,)), ((), ())), preferred_element_type=F32
             )
 
     def accumulate_two(o, _):
@@ -403,8 +401,8 @@
             pltpu.VMEM((2 * n_tm, 4, LANES), F32),
             pltpu.VMEM((4, LANES), F32),
             pltpu.VMEM((n_z, 4, LANES), F32),
-            pltpu.VMEM((SUBS, 4, 2 * BINS, QUARTERS * LANES), BF16),
-            pltpu.VMEM((SUBS, 4, QUARTERS, LANES), F32),
+            pltpu.VMEM((n_tm, 24, LANES), F32),
+            pltpu.VMEM((BINS, LANES), BF16),
             pltpu.VMEM((STEPS, 2 * BINS, 2 * LANES), F32),
             pltpu.VMEM((STEPS, 8, LANES), F32),
             pltpu.VMEM((STEPS, 8, LANES), F32),

time: 42.9 us -> 42.9 us (level)
  no operation moved by 1% of the time
where the time goes in v5:
time: 42.9 us; the launch traced here: 42.8 us
  Pallas kernels  42.2 us (98%)
  between operations  0.64 us (1%)
    pallas_call x1, Pallas kernels, local(): pl.pallas_call(functools.partial(kernel, n_tm, n_z), out_shape=(jax.Shape...  41.4 us

profile of v5, /device:TPU:1, one launch (start us, length us, event | category | flops | bytes accessed | tf_op | source)
XLA Modules:
  0.0 42.8 jit_solution(7155579482053127767)
XLA Ops:
  0.6 41.4 %shard_map.68 = (f32[16,32,32]{2,1,0:T(8,128)S(1)}, f32[16,4,128]{2,1,0:T(4,128)S(1)}) custom-call(s32[256,128]{1,0:T(8,128)} %bitcast.8, s32[8,128]{1,0:T(8,128)} %bitcast.9, f32[1,32]{1,0:T(1,128)} %bitcast.10, s32[1,32]{1,0:T(1,128)} %bitcast.11, s32[16]{0:T(128)} %roots_hbm.1), custom_call_target="tpu_custom_call" | custom-call | tf_op jit(solution)/shard_map/pallas_call | solution.py:377
  42.1 0.7 %shard_map.69 = (f32[16,32,32]{2,1,0:T(8,128)}, f32[16,32]{1,0:T(8,128)}) custom-call(f32[16,32,32]{2,1,0:T(8,128)S(1)} %get-tuple-element.4.split_ref, f32[16,4,128]{2,1,0:T(4,128)S(1)} %get-tuple-element.5.planes_ref), custom_call_target="tpu_custom_call" | custom-call | tf_op jit(solution)/shard_map/pallas_call | solution.py:423
